TPU v7x, 32 devices: a whole 2x2x4 slice. The times are simulated.
32 devices in a mesh: groups: 2 (over y), fsdp: 8 (over z, x), dp: 1, sub: 2 (over core).
Axes of the slice: x: 2, y: 2, z: 4, core: 2. Of those that a mesh axis runs over, the one named last changes fastest.
Arguments:
- features: bfloat16 [16, 768, 1280], P(('groups', 'fsdp', 'dp'), 'sub'), parts along dimension 0, may hold values from -6 to 6
- golden: bfloat16 [4, 768, 1280], P(('groups', 'dp'), 'sub'), parts along dimension 0, may hold values from -6 to 6
- die_wafer: int32 [16], P(('groups', 'fsdp', 'dp')), parts along dimension 0, may hold values from 0 to 1
- norm_gain: float32 [1280], replicated, may hold values from 0.1 to 1.9
- proj_weight: bfloat16 [1280, 2560], P('fsdp'), may hold values from -0.15625 to 0.15625
- out_weight: bfloat16 [2560, 1280], P('fsdp'), may hold values from -0.125 to 0.125
- zero_weight: bfloat16 [1280, 1280], P(None, 'fsdp'), may hold values from -0.15625 to 0.15625
Outputs:
- block_out: bfloat16 [16, 768, 1280], P(('groups', 'fsdp', 'dp'), 'sub'), parts along dimension 0
There are 2 independent parts, one for each index of `groups`. A program takes and returns all parts, laid end to end along the dimension named above; an argument that names none is the same for every part. Nothing has to cross between parts.
All inputs are finite; a program needn't handle non-finite values.
Results may differ from a plain program's by a relative error of at most 0.005.
Values may be sent and summed in bfloat16 or wider, within the bound.
A program may use at most 128 MiB of HBM per device.

v0:
```python
import jax
import jax.numpy as jnp
from jax import lax
from jax.sharding import PartitionSpec as P


def body(features, golden, die_wafer, norm_gain, proj_weight, out_weight, zero_weight):
    wafer_one = die_wafer[0]
    columns = jnp.einsum(
        "wpc,cd->wpd", golden, zero_weight, preferred_element_type=jnp.float32
    ).astype(jnp.bfloat16)
    gathered = lax.all_gather(columns, "fsdp", axis=2, tiled=True)
    residual = lax.dynamic_index_in_dim(gathered, wafer_one, 0, keepdims=False)
    mixed = features[0].astype(jnp.float32) + residual.astype(jnp.float32)
    average = jnp.mean(mixed, axis=-1, keepdims=True)
    centred = mixed - average
    variance = jnp.mean(centred * centred, axis=-1, keepdims=True)
    normed = (centred * lax.rsqrt(variance + 1e-05) * norm_gain).astype(jnp.bfloat16)
    inputs = normed
    preact = jnp.dot(
        inputs,
        lax.all_gather(proj_weight, "fsdp", axis=0, tiled=True),
        preferred_element_type=jnp.float32,
    )
    hidden = jax.nn.gelu(preact, approximate=True).astype(jnp.bfloat16)
    inputs = hidden
    branch = jnp.dot(
        inputs,
        lax.all_gather(out_weight, "fsdp", axis=0, tiled=True),
        preferred_element_type=jnp.float32,
    )
    return (mixed + branch).astype(jnp.bfloat16)[None]


def solution(mesh):
    placed = (
        P(("groups", "fsdp", "dp"), "sub", None),
        P(("groups", "dp"), "sub", None),
        P(("groups", "fsdp", "dp")),
        P(),
        P("fsdp", None),
        P("fsdp", None),
        P(None, "fsdp"),
    )
    return jax.shard_map(
        body,
        mesh=mesh,
        in_specs=placed,
        out_specs=P(("groups", "fsdp", "dp"), "sub", None),
        check_vma=False,
    )
```

profile of v0, /device:TPU:0, one launch (start us, length us, event | category | flops | bytes accessed | tf_op | source)
XLA Modules:
  0.0 289.0 jit_solution(17761163579044327469)
XLA Ops:
  6.5 0.0 copy-start
  6.5 0.0 all-gather.4.cloned.1.call-start
  6.5 1.5 copy-done
  8.1 2.5 convolution_convert_fusion
  10.6 0.0 all-gather.4.cloned.1.call-update
  10.6 0.0 all-gather.6.cloned.1.call-start
  10.7 0.7 all-gather.6.cloned.1.call-update
  11.4 0.0 all-gather.8.cloned.1.call-start
  11.4 0.7 all-gather.8.cloned.1.call-update
  12.7 1.6 copy.8
  14.3 46.6 %all-gather.4.cloned.1.call-done = bf16[2,384,1280]{1,2,0:T(8,128)(2,1)} async-done(((bf16[2,384,160]{1,2,0:T(8,128)(2,1)}), bf16[2,384,1280]{1,2,0:T(8,128)(2,1)}) %all-gather.4.cloned.1.call-update) | async-done | bytes 1966096 | tf_op jit(solution)/shard_map/all_gather | solution.py:12
  61.0 0.0 copy-start.1
  61.0 0.0 copy-start.2
  61.0 1.7 fusion.15
  62.7 0.1 copy-done.1
  62.8 0.4 multiply_reduce_fusion
  63.3 101.3 %all-gather.6.cloned.1.call-done = bf16[1280,2560]{1,0:T(8,128)(2,1)} async-done(((bf16[160,2560]{1,0:T(8,128)(2,1)}), bf16[1280,2560]{1,0:T(8,128)(2,1)}) %all-gather.6.cloned.1.call-update) | async-done | bytes 6553616 | tf_op jit(solution)/shard_map/all_gather | solution.py:22
  164.5 102.6 %all-gather.8.cloned.1.call-done = bf16[2560,1280]{1,0:T(8,128)(2,1)} async-done(((bf16[320,1280]{1,0:T(8,128)(2,1)}), bf16[2560,1280]{1,0:T(8,128)(2,1)}) %all-gather.8.cloned.1.call-update) | async-done | bytes 6553616 | tf_op jit(solution)/shard_map/all_gather | solution.py:29
  267.2 0.0 copy-done.2
  267.2 13.0 %fusion.9 = bf16[1,384,1280]{1,2,0:T(8,128)(2,1)} fusion(bf16[2560,1280]{1,0:T(8,128)(2,1)} %all-gather.8.cloned.1.call-done, bf16[1,384,1280]{1,2,0:T(8,128)(2,1)S(1)} %copy.8, bf16[1280,2560]{1,0:T(8,128)(2,1)} %all-gather.6.cloned.1.call-done, f32[1280]{0:T(1024)S(1)} %copy-done.2, f32[384]{0:T(512)S(1)} %add_rsqrt_fusion, ...), kind=kOutput, calls=%fused_computation.11 | convolution fusion | flops 5047910400 | bytes 18035712 | tf_op jit(solution)/shard_map/dot_general | solution.py:27
  280.2 2.2 copy.10
  (2 shorter events, 0.0 us)
Async XLA Ops:
  6.5 1.5 copy-start
  6.5 54.4 %all-gather.4.cloned.1.call-start = ((), (), s32[]{:S(2)}) async-start(), calls=%async_computation | async-start | bytes 2211840 | tf_op jit(solution)/shard_map/all_gather | solution.py:12
  10.6 153.9 %all-gather.6.cloned.1.call-start = ((), (), s32[]{:S(2)}) async-start(), calls=%async_computation.1 | async-start | bytes 7372800 | tf_op jit(solution)/shard_map/all_gather | solution.py:22
  11.4 255.8 %all-gather.8.cloned.1.call-start = ((), (), s32[]{:S(2)}) async-start(), calls=%async_computation.2 | async-start | bytes 7372800 | tf_op jit(solution)/shard_map/all_gather | solution.py:29
  61.0 1.8 copy-start.1
  61.0 206.2 %copy-start.2 = (f32[1280]{0:T(1024)S(1)}, f32[1280]{0:T(1024)}, u32[]{:S(2)}) copy-start(f32[1280]{0:T(1024)} %param.10) | copy-start | bytes 15364
Sparse Core Ops, SparseCore 0:
  10.7 50.2 all-gather.3
  63.2 101.3 all-gather.5
  166.7 100.3 all-gather.7
where the time goes:
time: 289 us
  waiting for transfers between devices  252 us (87%)
  matrix products  15.5 us (5%)
  between operations  13.8 us (5%)
  local copies, waits for them, and re-layouts  5.51 us (2%)
    all_gather x1, waiting for transfers between devices, body(): lax.all_gather(out_weight, 'fsdp', axis=0, tiled=True)  103 us
    all_gather x1, waiting for transfers between devices, body(): lax.all_gather(proj_weight, 'fsdp', axis=0, tiled=True)  101 us
    all_gather x1, waiting for transfers between devices, body(): gathered = lax.all_gather(columns, 'fsdp', axis=2, tiled=True)  46.6 us
    dot_general x1, matrix products, body(): jnp.dot(inputs, lax.all_gather(out_weight, 'fsdp', axis=0, tiled=True), p...  13 us
  transfers between devices with their start and end apart: 3, of which 3 were waited for; matrix products, arithmetic and copies ran while one was open for 1% of the time, Pallas kernels for 0%

commit v1 on v0

--- a/solution.py
+++ b/solution.py
@@ -2,6 +2,28 @@
 import jax.numpy as jnp
 from jax import lax
 from jax.sharding import PartitionSpec as P
+
+
+def laid_out(blocks, dim):
+    shape = list(blocks.shape[1:])
+    shape[dim] *= blocks.shape[0]
+    return jnp.moveaxis(blocks, 0, dim).reshape(shape)
+
+
+def gather_around(array, axis, dim):
+    size = lax.axis_size(axis)
+    pairs = [(i, (i + 1) % size) for i in range(size)]
+    back = [(b, a) for a, b in pairs]
+    lower, upper = ([], [])
+    for step in range(size - 1):
+        if step % 2 == 0:
+            lower.append(lax.ppermute(lower[-1] if lower else array, axis, pairs))
+        else:
+            upper.append(lax.ppermute(upper[-1] if upper else array, axis, back))
+    blocks = jnp.stack([*lower[::-1], array, *upper])
+    shift = lax.axis_index(axis) - len(lower)
+    blocks = blocks[(jnp.arange(size) - shift) % size]
+    return laid_out(blocks, dim)
 
 
 def body(features, golden, die_wafer, norm_gain, proj_weight, out_weight, zero_weight):
@@ -9,7 +31,7 @@
     columns = jnp.einsum(
         "wpc,cd->wpd", golden, zero_weight, preferred_element_type=jnp.float32
     ).astype(jnp.bfloat16)
-    gathered = lax.all_gather(columns, "fsdp", axis=2, tiled=True)
+    gathered = gather_around(columns, "fsdp", 2)
     residual = lax.dynamic_index_in_dim(gathered, wafer_one, 0, keepdims=False)
     mixed = features[0].astype(jnp.float32) + residual.astype(jnp.float32)
     average = jnp.mean(mixed, axis=-1, keepdims=True)

time: 289 us -> 252 us (0.87)
  waiting for transfers between devices: 252 us -> 190 us
  starting transfers between devices: 0.08 us -> 16.6 us
  local copies, waits for them, and re-layouts: 5.51 us -> 14.8 us
    all_gather x1, waiting for transfers between devices: 101 us -> 44.8 us  [body(): lax.all_gather(proj_weight, 'fsdp', axis=0, tiled=True)]
    all_gather x1 -> x0, waiting for transfers between devices: 46.6 us -> none  [body(): gathered = lax.all_gather(columns, 'fsdp', axis=2, tiled=True)]
    ppermute x0 -> x7, waiting for transfers between devices: none -> 41.6 us  [the longest x4 41 us: gather_around(): lower.append(lax.ppermute(lower[-1] if lower else array, axis, pairs))]
    ppermute x0 -> x7, starting transfers between devices: none -> 16.6 us  [the longest x3 11.7 us: gather_around(): upper.append(lax.ppermute(upper[-1] if upper else array, axis, back))]
    unnamed x7 -> x14, local copies, waits for them, and re-layouts: 3.28 us -> 7.64 us
    gather x0 -> x1, local copies, waits for them, and re-layouts: none -> 3.64 us  [gather_around(): blocks = blocks[(jnp.arange(size) - shift) % size]]
  transfers between devices with their start and end apart: 3 -> 9, of which waited for: 3 -> 7; matrix products, arithmetic and copies ran while one was open for 1% -> 7% of each run, Pallas kernels for 0% -> 0%
where the time goes in v1:
time: 252 us
  waiting for transfers between devices  190 us (75%)
  starting transfers between devices  16.6 us (7%)
  local copies, waits for them, and re-layouts  14.8 us (6%)
  between operations  14.1 us (6%)
  matrix products  13.5 us (5%)
    all_gather x1, waiting for transfers between devices, body(): lax.all_gather(out_weight, 'fsdp', axis=0, tiled=True)  103 us
    all_gather x1, waiting for transfers between devices, body(): lax.all_gather(proj_weight, 'fsdp', axis=0, tiled=True)  44.8 us
    ppermute x4, waiting for transfers between devices, gather_around(): lower.append(lax.ppermute(lower[-1] if lower else array, axis, pairs))  41 us
    ppermute x3, starting transfers between devices, gather_around(): upper.append(lax.ppermute(upper[-1] if upper else array, axis, back))  11.7 us
    dot_general x1, matrix products, body(): jnp.dot(inputs, lax.all_gather(out_weight, 'fsdp', axis=0, tiled=True), p...  11.7 us
    unnamed x14, local copies, waits for them, and re-layouts  7.64 us
  transfers between devices with their start and end apart: 9, of which 7 were waited for; matrix products, arithmetic and copies ran while one was open for 7% of the time, Pallas kernels for 0%

profile of v1, /device:TPU:0, one launch (start us, length us, event | category | flops | bytes accessed | tf_op | source)
XLA Modules:
  0.0 251.6 jit_solution(8641852326645881122)
XLA Ops:
  8.1 1.8 convolution_convert_fusion
  9.9 3.0 %collective-permute-start = (bf16[2,384,160]{1,2,0:T(8,128)(2,1)S(1)}, bf16[2,384,160]{1,2,0:T(8,128)(2,1)S(1)}, u32[]{:S(2)}, u32[]{:S(2)}) collective-permute-start(bf16[2,384,160]{1,2,0:T(8,128)(2,1)S(1)} %convolution_convert_fusion), channel_id=1, source_target_pairs={{0,2},{2,4},{4,6},{6,8},{8,10},{10,12},{12,14},{14,0},{1,3},{3,5},... | collective-permute-start | bytes 737288 | tf_op jit(solution)/shard_map/ppermute | solution.py:20
  12.9 9.0 %collective-permute-done = bf16[2,384,160]{1,2,0:T(8,128)(2,1)S(1)} collective-permute-done((bf16[2,384,160]{1,2,0:T(8,128)(2,1)S(1)}, bf16[2,384,160]{1,2,0:T(8,128)(2,1)S(1)}, u32[]{:S(2)}, u32[]{:S(2)}) %collective-permute-start) | collective-permute-done | bytes 245792 | tf_op jit(solution)/shard_map/ppermute | solution.py:20
  21.9 4.7 %collective-permute-start.4 = (bf16[2,384,160]{1,2,0:T(8,128)(2,1)S(1)}, bf16[2,384,160]{1,2,0:T(8,128)(2,1)S(1)}, u32[]{:S(2)}, u32[]{:S(2)}) collective-permute-start(bf16[2,384,160]{1,2,0:T(8,128)(2,1)S(1)} %convolution_convert_fusion), channel_id=1, source_target_pairs={{2,0},{4,2},{6,4},{8,6},{10,8},{12,10},{14,12},{0,14},{3,1},{5,3},... | collective-permute-start | bytes 737288 | tf_op jit(solution)/shard_map/ppermute | solution.py:22
  26.6 11.4 %collective-permute-done.1 = bf16[2,384,160]{1,2,0:T(8,128)(2,1)S(1)} collective-permute-done((bf16[2,384,160]{1,2,0:T(8,128)(2,1)S(1)}, bf16[2,384,160]{1,2,0:T(8,128)(2,1)S(1)}, u32[]{:S(2)}, u32[]{:S(2)}) %collective-permute-start.1) | collective-permute-done | bytes 245792 | tf_op jit(solution)/shard_map/ppermute | solution.py:20
  38.0 1.9 collective-permute-start.2
  40.5 2.2 collective-permute-start.5
  42.8 11.3 %collective-permute-done.2 = bf16[2,384,160]{1,2,0:T(8,128)(2,1)S(1)} collective-permute-done((bf16[2,384,160]{1,2,0:T(8,128)(2,1)S(1)}, bf16[2,384,160]{1,2,0:T(8,128)(2,1)S(1)}, u32[]{:S(2)}, u32[]{:S(2)}) %collective-permute-start.2) | collective-permute-done | bytes 245792 | tf_op jit(solution)/shard_map/ppermute | solution.py:20
  54.7 4.8 %collective-permute-start.6 = (bf16[2,384,160]{1,2,0:T(8,128)(2,1)S(1)}, bf16[2,384,160]{1,2,0:T(8,128)(2,1)S(1)}, u32[]{:S(2)}, u32[]{:S(2)}) collective-permute-start(bf16[2,384,160]{1,2,0:T(8,128)(2,1)S(1)} %collective-permute-done.5), channel_id=1, source_target_pairs={{2,0},{4,2},{6,4},{8,6},{10,8},{12,10},{14,12},{0,14},{3,1},{5,3},... | collective-permute-start | bytes 737288 | tf_op jit(solution)/shard_map/ppermute | solution.py:22
  59.5 9.3 %collective-permute-done.3 = bf16[2,384,160]{1,2,0:T(8,128)(2,1)} collective-permute-done((bf16[2,384,160]{1,2,0:T(8,128)(2,1)S(1)}, bf16[2,384,160]{1,2,0:T(8,128)(2,1)}, u32[]{:S(2)}, u32[]{:S(2)}) %collective-permute-start.3) | collective-permute-done | bytes 245792 | tf_op jit(solution)/shard_map/ppermute | solution.py:20
  68.8 1.7 bitcast_dynamic-update-slice_fusion.7
  70.5 0.7 bitcast_dynamic-update-slice_fusion.6
  71.2 0.7 bitcast_dynamic-update-slice_fusion.5
  71.9 0.7 bitcast_dynamic-update-slice_fusion.4
  74.1 0.7 bitcast_dynamic-update-slice_fusion.1
  74.8 0.7 bitcast_dynamic-update-slice_fusion
  75.5 3.6 %gather_fusion = bf16[8,2,384,160]{2,3,1,0:T(8,128)(2,1)} fusion(bf16[8,2,384,160]{2,3,1,0:T(8,128)(2,1)} %bitcast_dynamic-update-slice_fusion, s32[1024]{0:T(1024)S(1)} %pad_clamp_fusion), kind=kCustom, calls=%fused_computation | custom fusion | bytes 3932192 | tf_op jit(solution)/shard_map/gather | solution.py:25
  79.2 1.7 copy.8
  80.9 1.1 constant_dynamic-slice_fusion
  82.0 1.5 copy.10
  83.6 1.6 fusion.15
  85.7 44.8 %all-gather.3.cloned.1.call-done = bf16[1280,2560]{1,0:T(8,128)(2,1)} async-done(((bf16[160,2560]{1,0:T(8,128)(2,1)}), bf16[1280,2560]{1,0:T(8,128)(2,1)}) %all-gather.3.cloned.1.call-update) | async-done | bytes 6553616 | tf_op jit(solution)/shard_map/all_gather | solution.py:44
  130.5 102.6 %all-gather.5.cloned.1.call-done = bf16[2560,1280]{1,0:T(8,128)(2,1)} async-done(((bf16[320,1280]{1,0:T(8,128)(2,1)}), bf16[2560,1280]{1,0:T(8,128)(2,1)}) %all-gather.5.cloned.1.call-update) | async-done | bytes 6553616 | tf_op jit(solution)/shard_map/all_gather | solution.py:51
  233.1 11.7 %fusion.9 = bf16[1,384,1280]{2,1,0:T(8,128)(2,1)} fusion(bf16[2560,1280]{1,0:T(8,128)(2,1)} %all-gather.5.cloned.1.call-done, bf16[1,384,1280]{2,1,0:T(8,128)(2,1)S(1)} %copy.10, bf16[1,384,1280]{2,1,0:T(8,128)(2,1)} %param.7, bf16[1280,2560]{1,0:T(8,128)(2,1)} %all-gather.3.cloned.1.call-done, f32[1280]{0:T(1024)S(1)} %copy-done.2, ...), kind=kOutput, calls=%fused_computation.12 | convolution fusion | flops 5047910400 | bytes 16064512 | tf_op jit(solution)/shard_map/dot_general | solution.py:49
  (22 shorter events, 4.1 us)
Async XLA Ops:
  6.5 1.5 copy-start
  6.5 123.9 %all-gather.3.cloned.1.call-start = ((), (), s32[]{:S(2)}) async-start(), calls=%async_computation | async-start | bytes 7372800 | tf_op jit(solution)/shard_map/all_gather | solution.py:44
  7.3 225.8 %all-gather.5.cloned.1.call-start = ((), (), s32[]{:S(2)}) async-start(), calls=%async_computation.1 | async-start | bytes 7372800 | tf_op jit(solution)/shard_map/all_gather | solution.py:51
  9.9 12.0 %collective-permute-start = (bf16[2,384,160]{1,2,0:T(8,128)(2,1)S(1)}, bf16[2,384,160]{1,2,0:T(8,128)(2,1)S(1)}, u32[]{:S(2)}, u32[]{:S(2)}) collective-permute-start(bf16[2,384,160]{1,2,0:T(8,128)(2,1)S(1)} %convolution_convert_fusion), channel_id=1, source_target_pairs={{0,2},{2,4},{4,6},{6,8},{8,10},{10,12},{12,14},{14,0},{1,3},{3,5},... | collective-permute-start | bytes 737288 | tf_op jit(solution)/shard_map/ppermute | solution.py:20
  21.9 16.2 %collective-permute-start.1 = (bf16[2,384,160]{1,2,0:T(8,128)(2,1)S(1)}, bf16[2,384,160]{1,2,0:T(8,128)(2,1)S(1)}, u32[]{:S(2)}, u32[]{:S(2)}) collective-permute-start(bf16[2,384,160]{1,2,0:T(8,128)(2,1)S(1)} %collective-permute-done), channel_id=1, source_target_pairs={{0,2},{2,4},{4,6},{6,8},{8,10},{10,12},{12,14},{14,0},{1,3},{3,5},... | collective-permute-start | bytes 737288 | tf_op jit(solution)/shard_map/ppermute | solution.py:20
  21.9 18.7 %collective-permute-start.4 = (bf16[2,384,160]{1,2,0:T(8,128)(2,1)S(1)}, bf16[2,384,160]{1,2,0:T(8,128)(2,1)S(1)}, u32[]{:S(2)}, u32[]{:S(2)}) collective-permute-start(bf16[2,384,160]{1,2,0:T(8,128)(2,1)S(1)} %convolution_convert_fusion), channel_id=1, source_target_pairs={{2,0},{4,2},{6,4},{8,6},{10,8},{12,10},{14,12},{0,14},{3,1},{5,3},... | collective-permute-start | bytes 737288 | tf_op jit(solution)/shard_map/ppermute | solution.py:22
  38.0 16.0 %collective-permute-start.2 = (bf16[2,384,160]{1,2,0:T(8,128)(2,1)S(1)}, bf16[2,384,160]{1,2,0:T(8,128)(2,1)S(1)}, u32[]{:S(2)}, u32[]{:S(2)}) collective-permute-start(bf16[2,384,160]{1,2,0:T(8,128)(2,1)S(1)} %collective-permute-done.1), channel_id=1, source_target_pairs={{0,2},{2,4},{4,6},{6,8},{8,10},{10,12},{12,14},{14,0},{1,3},{3,5},... | collective-permute-start | bytes 737288 | tf_op jit(solution)/shard_map/ppermute | solution.py:20
  40.5 14.2 %collective-permute-start.5 = (bf16[2,384,160]{1,2,0:T(8,128)(2,1)S(1)}, bf16[2,384,160]{1,2,0:T(8,128)(2,1)S(1)}, u32[]{:S(2)}, u32[]{:S(2)}) collective-permute-start(bf16[2,384,160]{1,2,0:T(8,128)(2,1)S(1)} %collective-permute-done.4), channel_id=1, source_target_pairs={{2,0},{4,2},{6,4},{8,6},{10,8},{12,10},{14,12},{0,14},{3,1},{5,3},... | collective-permute-start | bytes 737288 | tf_op jit(solution)/shard_map/ppermute | solution.py:22
  54.0 14.8 %collective-permute-start.3 = (bf16[2,384,160]{1,2,0:T(8,128)(2,1)S(1)}, bf16[2,384,160]{1,2,0:T(8,128)(2,1)}, u32[]{:S(2)}, u32[]{:S(2)}) collective-permute-start(bf16[2,384,160]{1,2,0:T(8,128)(2,1)S(1)} %collective-permute-done.2), channel_id=1, source_target_pairs={{0,2},{2,4},{4,6},{6,8},{8,10},{10,12},{12,14},{14,0},{1,3},{3,5},... | collective-permute-start | bytes 737288 | tf_op jit(solution)/shard_map/ppermute | solution.py:20
  54.7 20.1 %collective-permute-start.6 = (bf16[2,384,160]{1,2,0:T(8,128)(2,1)S(1)}, bf16[2,384,160]{1,2,0:T(8,128)(2,1)S(1)}, u32[]{:S(2)}, u32[]{:S(2)}) collective-permute-start(bf16[2,384,160]{1,2,0:T(8,128)(2,1)S(1)} %collective-permute-done.5), channel_id=1, source_target_pairs={{2,0},{4,2},{6,4},{8,6},{10,8},{12,10},{14,12},{0,14},{3,1},{5,3},... | collective-permute-start | bytes 737288 | tf_op jit(solution)/shard_map/ppermute | solution.py:22
  83.5 1.7 copy-start.1
  83.6 149.5 %copy-start.2 = (f32[1280]{0:T(1024)S(1)}, f32[1280]{0:T(1024)}, u32[]{:S(2)}) copy-start(f32[1280]{0:T(1024)} %param.10) | copy-start | bytes 15364
Sparse Core Ops, SparseCore 0:
  9.5 120.8 all-gather.2
  132.6 100.3 all-gather.4
